TPU v7x, 32 devices: a whole 2x2x4 slice. The times are simulated.
32 devices in a mesh: dp: 16 (over z, y, core), seq: 2 (over x).
Axes of the slice: x: 2, y: 2, z: 4, core: 2. Of those that a mesh axis runs over, the one named last changes fastest.
Arguments:
- tokens: bfloat16 [16, 256, 8192], P('dp', None, 'seq'), may hold values from -6 to 6
- queries: bfloat16 [16, 256, 1024], P('dp', 'seq'), may hold values from -96 to 96
- grad_out: bfloat16 [16, 256, 1024], P('dp', 'seq'), may hold values from -6 to 6
- w_kv: bfloat16 [8192, 256], P('seq'), may hold values from -0.0625 to 0.0625
- doc_ids: int32 [16, 256], P('dp'), may hold values from 0 to 5, never falling along the last dimension, each value on 1 to 85 neighbouring positions
- span_order: int32 [2], replicated, may hold values from 0 to 1, each once
Outputs:
- attention: bfloat16 [16, 256, 1024], P('dp', 'seq')
- query_grad: bfloat16 [16, 256, 1024], P('dp', 'seq')
- weight_grad: bfloat16 [8192, 256], P('seq')
Inputs may be any that keep to these rules, and one draw needn't show every extreme that they name: `doc_ids`: document ids never fall along positions; every id is used; a document holds at most 85 positions. `span_order`: each block index appears once.
All inputs are finite; a program needn't handle non-finite values.
Results may differ from a plain program's by a relative error of at most 0.007.
The roundings to bfloat16 on the way count: a program that leaves them out, or rounds other values in their place, can miss the bound.
Values may be sent and summed in bfloat16 or wider, within the bound.
No kernel may reach another device: no remote copies, remote signals or barrier semaphores. Data moves between devices by JAX's collectives and lax.ppermute only.
A program may use at most 64 MiB of HBM per device.

v0:
```python
import math

import jax
import jax.numpy as jnp
from jax import lax
from jax.sharding import PartitionSpec as P

HEAD = 128
QH = 8


def per_device(tokens, queries, grad_out, w_kv, doc_ids, span_order):
    rows_dev = queries.shape[1]
    seq_len = tokens.shape[1]
    pack_count = queries.shape[0]
    seq_index = lax.axis_index("seq")
    span_count = span_order.shape[0]
    row_ids = jnp.arange(seq_len, dtype=jnp.int32)
    owners = row_ids // rows_dev
    selector = (owners[:, None] == jnp.arange(span_count, dtype=jnp.int32)[None, :]).astype(
        jnp.int32
    )
    span_of = jnp.sum(selector * span_order[None, :], axis=1)
    positions = span_of * rows_dev + row_ids % rows_dev
    own_pos = lax.dynamic_slice_in_dim(positions, seq_index * rows_dev, rows_dev, 0)
    doc_rows = jnp.take(doc_ids, positions, axis=1)
    own_docs = lax.dynamic_slice_in_dim(doc_rows, seq_index * rows_dev, rows_dev, 1)
    allowed = (positions[None, None, :] <= own_pos[None, :, None]) & (
        doc_rows[:, None, :] == own_docs[:, :, None]
    )
    allowed = allowed[:, None]
    flat_tokens = tokens[0]
    own_rows = lax.psum_scatter(
        jnp.dot(flat_tokens, w_kv, preferred_element_type=jnp.float32),
        "seq",
        scatter_dimension=0,
        tiled=True,
    ).astype(jnp.bfloat16)
    key_value = lax.all_gather(own_rows[None], "seq", axis=1, tiled=True)
    key_part = key_value[..., :HEAD]
    value_part = key_value[..., HEAD:]
    score_scale = 1.0 / math.sqrt(HEAD)
    query_heads = queries.reshape(pack_count, rows_dev, QH, HEAD)
    grad_heads = grad_out.reshape(pack_count, rows_dev, QH, HEAD)
    scores = (
        jnp.einsum("bqhe,bke->bhqk", query_heads, key_part, preferred_element_type=jnp.float32)
        * score_scale
    )
    scores = jnp.where(allowed, scores, jnp.float32(-1e30))
    top_score = jnp.max(scores, axis=-1, keepdims=True)
    expo = jnp.exp(scores - top_score)
    attn_probs = expo / jnp.sum(expo, axis=-1, keepdims=True)
    probs_low = attn_probs.astype(jnp.bfloat16)
    attended = jnp.einsum(
        "bhqk,bke->bqhe", probs_low, value_part, preferred_element_type=jnp.float32
    )
    attention = attended.astype(jnp.bfloat16).reshape(queries.shape)
    grad_probs = jnp.einsum(
        "bqhe,bke->bhqk", grad_heads, value_part, preferred_element_type=jnp.float32
    )
    row_delta = jnp.sum(attn_probs * grad_probs, axis=-1, keepdims=True)
    grad_scores = (attn_probs * (grad_probs - row_delta) * score_scale).astype(jnp.bfloat16)
    query_grad = jnp.einsum(
        "bhqk,bke->bqhe", grad_scores, key_part, preferred_element_type=jnp.float32
    )
    query_grad = query_grad.astype(jnp.bfloat16).reshape(queries.shape)
    key_grad = jnp.einsum(
        "bhqk,bqhe->bke", grad_scores, query_heads, preferred_element_type=jnp.float32
    )
    value_grad = jnp.einsum(
        "bhqk,bqhe->bke", probs_low, grad_heads, preferred_element_type=jnp.float32
    )
    grad_terms = jnp.concatenate([key_grad, value_grad], axis=-1)
    grad_kv = lax.psum(grad_terms, "seq").astype(jnp.bfloat16)
    weight_part = jnp.einsum("bsd,bsc->dc", tokens, grad_kv, preferred_element_type=jnp.float32)
    weight_total = lax.psum(weight_part, "dp")
    weight_grad = (weight_total / lax.axis_size("dp")).astype(jnp.bfloat16)
    return (attention, query_grad, weight_grad)


def solution(mesh):
    return jax.shard_map(
        per_device,
        mesh=mesh,
        in_specs=(
            P("dp", None, "seq"),
            P("dp", "seq", None),
            P("dp", "seq", None),
            P("seq", None),
            P("dp", None),
            P(),
        ),
        out_specs=(P("dp", "seq", None), P("dp", "seq", None), P("seq", None)),
        check_vma=False,
    )
```

profile of v0, /device:TPU:0, one launch (start us, length us, event | category | flops | bytes accessed | tf_op | source)
XLA Modules:
  0.0 176.2 jit_solution(15871811188909200683)
XLA Ops:
  7.2 0.0 reduce-scatter.2.cloned.1.call-start
  7.3 1.5 copy-done
  8.8 3.0 %fusion.1 = f32[256,256]{1,0:T(8,128)} fusion(bf16[4096,256]{1,0:T(8,128)(2,1)} %param.9, bf16[1,256,4096]{2,1,0:T(8,128)(2,1)S(1)} %copy-done), kind=kOutput, calls=%fused_computation.4 | convolution fusion | flops 536870912 | bytes 4456448 | tf_op jit(solution)/shard_map/dot_general | solution.py:34
  11.8 0.0 reduce-scatter.2.cloned.1.call-update
  11.8 0.0 all-reduce.3.cloned.1.call-start
  11.9 0.1 fusion.14
  12.0 1.9 %gather_fusion = s32[256]{0:T(256)S(1)} fusion(s32[256]{0:T(256)S(1)} %bitcast.78, s32[1024]{0:T(1024)S(1)} %pad_clamp_fusion), kind=kCustom, calls=%fused_computation | custom fusion | bytes 3072 | tf_op jit(solution)/shard_map/jit(_take)/gather | solution.py:26
  14.0 0.2 copy.56
  14.1 0.8 copy.57
  15.0 0.1 dynamic_slice.6
  15.1 0.1 compare_and_fusion
  15.2 11.1 %reduce-scatter.2.cloned.1.call-done = f32[128,256]{1,0:T(8,128)} async-done(((f32[256,256]{1,0:T(8,128)}), f32[128,256]{1,0:T(8,128)}) %reduce-scatter.2.cloned.1.call-update) | async-done | bytes 131088 | tf_op jit(solution)/shard_map/reduce_scatter | solution.py:33
  26.3 1.0 convert_element_type.34
  27.3 4.9 %all-gather = bf16[256,256]{1,0:T(8,128)(2,1)S(1)} all-gather(bf16[128,256]{1,0:T(8,128)(2,1)S(1)} %convert_element_type.34), channel_id=2, replica_groups=mesh['dp'=16,'seq'=2] {'seq'}, dimensions={0}, use_global_device_ids=true | all-gather | bytes 196608 | tf_op jit(solution)/shard_map/all_gather | solution.py:39
  32.2 0.3 fusion.24
  32.5 0.2 fusion.6
  32.7 0.3 convolution_bitcast_fusion.2
  33.0 0.3 multiply_reduce_fusion
  33.4 0.3 fusion.7
  33.7 0.8 copy-done.2
  34.4 0.3 convolution_bitcast_fusion.3
  34.8 10.5 %all-reduce.4 = bf16[1,256,256]{1,2,0:T(8,128)(2,1)S(1)} all-reduce(f32[1,256,256]{1,2,0:T(8,128)S(1)} %pad_maximum_fusion), channel_id=1, replica_groups=mesh['dp'=16,'seq'=2] {'seq'}, use_global_device_ids=true, to_apply=%region_5.6 | all-reduce | flops 65536 | bytes 393216 | tf_op jit(solution)/shard_map/psum | solution.py:74
  45.3 2.7 %convolution_bitcast_fusion = f32[4096,256]{0,1:T(8,128)} fusion(bf16[1,256,4096]{2,1,0:T(8,128)(2,1)S(1)} %copy-done, bf16[1,256,256]{1,2,0:T(8,128)(2,1)S(1)} %all-reduce.4), kind=kOutput, calls=%fused_computation.1 | convolution fusion | flops 536870912 | bytes 6422528 | tf_op jit(solution)/shard_map/bsd,bsc->dc/dot_general | solution.py:75
  48.0 0.0 all-reduce.3.cloned.1.call-update
  48.0 0.9 copy-done.4
  48.9 0.3 convolution_convert_fusion.1
  49.2 0.9 copy.45
  50.1 1.3 convolution_convert_fusion
  51.4 0.9 copy.46
  52.2 109.2 %all-reduce.3.cloned.1.call-done = f32[4096,256]{0,1:T(8,128)} async-done(((f32[4096,256]{0,1:T(8,128)}), f32[4096,256]{0,1:T(8,128)}) %all-reduce.3.cloned.1.call-update) | async-done | bytes 4194320 | tf_op jit(solution)/shard_map/psum | solution.py:76
  161.4 3.9 %multiply_convert_fusion = bf16[4096,256]{0,1:T(8,128)(2,1)} fusion(f32[4096,256]{0,1:T(8,128)} %all-reduce.3.cloned.1.call-done), kind=kLoop, calls=%fused_computation.2 | loop fusion | flops 2097152 | bytes 6291456 | tf_op jit(solution)/shard_map/convert_element_type | solution.py:77
  165.3 4.1 %copy.47 = bf16[4096,256]{1,0:T(8,128)(2,1)} copy(bf16[4096,256]{0,1:T(8,128)(2,1)} %multiply_convert_fusion) | data formatting | bytes 4194304
  (23 shorter events, 0.1 us)
Async XLA Ops:
  7.2 1.6 copy-start
  7.2 4.7 %copy-start.8 = (s32[2]{0:T(128)S(1)}, s32[2]{0:T(128)}, u32[]{:S(2)}) copy-start(s32[2]{0:T(128)} %param.11) | copy-start | bytes 28
  7.2 4.8 %copy-start.1 = (s32[1,256]{1,0:T(1,128)S(1)}, s32[1,256]{1,0:T(1,128)}, u32[]{:S(2)}) copy-start(s32[1,256]{1,0:T(1,128)} %param.10) | copy-start | bytes 3076
  7.2 6.8 %copy-start.5 = (bf16[1,128,1024]{2,1,0:T(8,128)(2,1)S(1)}, bf16[1,128,1024]{2,1,0:T(8,128)(2,1)}, u32[]{:S(2)}) copy-start(bf16[1,128,1024]{2,1,0:T(8,128)(2,1)} %param.7) | copy-start | bytes 786436
  7.2 6.9 %copy-start.6 = (bf16[1,128,1024]{2,1,0:T(8,128)(2,1)S(1)}, bf16[1,128,1024]{2,1,0:T(8,128)(2,1)}, u32[]{:S(2)}) copy-start(bf16[1,128,1024]{2,1,0:T(8,128)(2,1)} %param.8) | copy-start | bytes 786436
  7.2 19.1 %reduce-scatter.2.cloned.1.call-start = ((), (), s32[]{:S(2)}) async-start(), calls=%async_computation.1 | async-start | bytes 393216 | tf_op jit(solution)/shard_map/reduce_scatter | solution.py:33
  11.8 149.6 %all-reduce.3.cloned.1.call-start = ((), (), s32[]{:S(2)}) async-start(), calls=%async_computation.2 | async-start | bytes 8388608 | tf_op jit(solution)/shard_map/psum | solution.py:76
  26.3 6.4 %copy-start.7 = (bf16[1,128,1024]{1,2,0:T(8,128)(2,1)S(1)}, bf16[1,128,1024]{1,2,0:T(8,128)(2,1)}, u32[]{:S(2)}) copy-start(bf16[1,128,1024]{1,2,0:T(8,128)(2,1)} %copy.57) | copy-start | bytes 786436
  32.2 0.8 copy-start.3
  33.6 0.8 copy-start.2
  48.0 0.9 copy-start.4
Sparse Core Ops, SparseCore 0:
  11.9 14.3 reduce-scatter.1
  48.1 113.2 all-reduce.2
where the time goes:
time: 177 us; the launch traced here: 176 us
  waiting for transfers between devices  120 us (68%)
  blocking collectives  15.4 us (9%)
  between operations  14.3 us (8%)
  local copies, waits for them, and re-layouts  12 us (7%)
  matrix products  8.55 us (5%)
  other arithmetic  5.54 us (3%)
    psum x1, waiting for transfers between devices, per_device(): weight_total = lax.psum(weight_part, 'dp')  109 us
    reduce_scatter x1, waiting for transfers between devices, per_device(): lax.psum_scatter(jnp.dot(flat_tokens, w_kv, preferred_element_type=jnp.fl...  11.1 us
    psum x1, blocking collectives, per_device(): grad_kv = lax.psum(grad_terms, 'seq').astype(jnp.bfloat16)  10.5 us
    unnamed x21, local copies, waits for them, and re-layouts  8.96 us
    all_gather x1, blocking collectives, per_device(): key_value = lax.all_gather(own_rows[None], 'seq', axis=1, tiled=True)  4.94 us
    convert_element_type x1, other arithmetic, per_device(): weight_grad = (weight_total / lax.axis_size('dp')).astype(jnp.bfloat16)  3.85 us
  transfers between devices with their start and end apart: 2, of which 2 were waited for; matrix products, arithmetic and copies ran while one was open for 4% of the time, Pallas kernels for 0%

commit v1 on v0

v1 whole, which is shorter than its diff:
```python
import functools
import math

import jax
import jax.numpy as jnp
from jax import lax
from jax.experimental import pallas as pl
from jax.experimental.pallas import tpu as pltpu
from jax.sharding import PartitionSpec as P

HEAD = 128
QH = 8
GROUP = 2
F32 = jnp.float32
BF16 = jnp.bfloat16
NT = (((1,), (1,)), ((), ()))
TN = (((0,), (0,)), ((), ()))
NN = (((1,), (0,)), ((), ()))


def _mm(a, b, dims):
    return lax.dot_general(a, b, dims, preferred_element_type=F32)


def attention_kernel(parts, own, order_ref, docs_ref, q_ref, g_ref, *refs):
    kv_refs = refs[:parts]
    att_ref, qg_ref, kvg_ref = refs[parts:]
    rows = q_ref.shape[0]
    seq_len = kv_refs[0].shape[0]
    spans = seq_len // rows
    if parts == 1:
        kv = kv_refs[0][...]
    else:
        kv = (kv_refs[0][...] + kv_refs[1][...]).astype(BF16)
    keys = kv[:, :HEAD]
    values = kv[:, HEAD:]
    keys_t = keys.T
    values_t = values.T
    scale = 1.0 / math.sqrt(HEAD)
    me = lax.axis_index(own)

    def row_docs(span):
        return docs_ref[pl.ds(order_ref[span], 1), :]

    masks = []
    q_docs = row_docs(me)
    q_span = order_ref[me]
    q_pos = lax.broadcasted_iota(jnp.int32, (rows, rows), 1)
    k_pos = lax.broadcasted_iota(jnp.int32, (rows, rows), 0)
    for span in range(spans):
        k_docs = jnp.broadcast_to(row_docs(span), (rows, rows)).T
        gap = (order_ref[span] - q_span) * rows
        masks.append((k_pos + gap <= q_pos) & (k_docs == q_docs))
    allowed = jnp.concatenate(masks, axis=0)
    allowed = jnp.concatenate([allowed] * GROUP, axis=1)

    key_grad = jnp.zeros((seq_len, HEAD), F32)
    value_grad = jnp.zeros((seq_len, HEAD), F32)
    for first in range(0, QH, GROUP):
        heads = range(first, first + GROUP)
        q = jnp.concatenate([q_ref[:, h * HEAD : (h + 1) * HEAD] for h in heads], axis=0)
        g = jnp.concatenate([g_ref[:, h * HEAD : (h + 1) * HEAD] for h in heads], axis=0)
        scores = jnp.where(allowed, _mm(keys, q, NT) * scale, F32(-1e30))
        expo = jnp.exp(scores - jnp.max(scores, axis=0, keepdims=True))
        probs = expo * (1.0 / jnp.sum(expo, axis=0, keepdims=True))
        low = probs.astype(BF16)
        grad_probs = _mm(values, g, NT)
        delta = jnp.sum(probs * grad_probs, axis=0, keepdims=True)
        grad_scores = (probs * (grad_probs - delta) * scale).astype(BF16)
        att = _mm(values_t, low, NN)
        qg = _mm(keys_t, grad_scores, NN)
        for i, h in enumerate(heads):
            cols = slice(h * HEAD, (h + 1) * HEAD)
            att_ref[:, cols] = att[:, i * rows : (i + 1) * rows].T.astype(BF16)
            qg_ref[:, cols] = qg[:, i * rows : (i + 1) * rows].T.astype(BF16)
        key_grad += _mm(grad_scores, q, NN)
        value_grad += _mm(low, g, NN)
    kvg_ref[:, :HEAD] = key_grad
    kvg_ref[:, HEAD:] = value_grad


def attend(order, docs, q, g, kvs):
    vmem = pl.BlockSpec(memory_space=pltpu.VMEM)
    return pl.pallas_call(
        functools.partial(attention_kernel, len(kvs), "seq"),
        out_shape=(
            jax.ShapeDtypeStruct(q.shape, BF16),
            jax.ShapeDtypeStruct(q.shape, BF16),
            jax.ShapeDtypeStruct((kvs[0].shape[0], 2 * HEAD), F32),
        ),
        in_specs=[pl.BlockSpec(memory_space=pltpu.SMEM)] + [vmem] * (3 + len(kvs)),
        out_specs=(vmem, vmem, vmem),
        compiler_params=pltpu.CompilerParams(vmem_limit_bytes=48 * 1024 * 1024),
        name="attention_fwd_bwd",
    )(order, docs, q, g, *kvs)


def per_device(tokens, queries, grad_out, w_kv, doc_ids, span_order):
    seq_size = lax.axis_size("seq")
    dp_size = lax.axis_size("dp")
    rows_dev = queries.shape[1]
    flat = tokens[0]
    spread = lax.all_to_all(flat, "dp", split_axis=1, concat_axis=0, tiled=True)
    partial = jnp.dot(flat, w_kv, preferred_element_type=F32)
    swap = [(i, i ^ 1) for i in range(2)]
    if seq_size == 2:
        kvs = [partial, lax.ppermute(partial, "seq", swap)]
    else:
        own = lax.psum_scatter(partial, "seq", scatter_dimension=0, tiled=True).astype(BF16)
        kvs = [lax.all_gather(own, "seq", axis=0, tiled=True)]
    docs = doc_ids.reshape(-1, rows_dev)
    attention, query_grad, terms = attend(span_order, docs, queries[0], grad_out[0], kvs)
    if seq_size == 2:
        grad_kv = (terms + lax.ppermute(terms, "seq", swap)).astype(BF16)
    else:
        grad_kv = lax.psum(terms, "seq").astype(BF16)
    all_grads = lax.all_gather(grad_kv, "dp", axis=0, tiled=True)
    piece = _mm(spread, all_grads, TN)
    piece = (piece * (1.0 / dp_size)).astype(BF16)
    weight_grad = lax.all_gather(piece, "dp", axis=0, tiled=True)
    return (attention[None], query_grad[None], weight_grad)


def solution(mesh):
    return jax.shard_map(
        per_device,
        mesh=mesh,
        in_specs=(
            P("dp", None, "seq"),
            P("dp", "seq", None),
            P("dp", "seq", None),
            P("seq", None),
            P("dp", None),
            P(),
        ),
        out_specs=(P("dp", "seq", None), P("dp", "seq", None), P("seq", None)),
        check_vma=False,
    )
```

time: 177 us -> 155 us (0.88)
  blocking collectives: 15.4 us -> 0 us
  waiting for transfers between devices: 120 us -> 106 us
  starting transfers between devices: 0.08 us -> 10.8 us
  other arithmetic: 5.54 us -> 0.68 us
  Pallas kernels: 0 us -> 3.23 us
  matrix products: 8.55 us -> 5.96 us
    psum x1 -> x0, waiting for transfers between devices: 109 us -> none  [per_device(): weight_total = lax.psum(weight_part, 'dp')]
    all_gather x0 -> x2, waiting for transfers between devices: none -> 55.3 us  [the longest x1 43.2 us: per_device(): weight_grad = lax.all_gather(piece, 'dp', axis=0, tiled=True)]
    all_to_all x0 -> x1, waiting for transfers between devices: none -> 44.6 us  [per_device(): spread = lax.all_to_all(flat, 'dp', split_axis=1, concat_axis=0, tiled=True)]
    reduce_scatter x1 -> x0, waiting for transfers between devices: 11.1 us -> none  [per_device(): lax.psum_scatter(jnp.dot(flat_tokens, w_kv, preferred_element_type=jnp.fl...]
    psum x1 -> x0, blocking collectives: 10.5 us -> none  [per_device(): grad_kv = lax.psum(grad_terms, 'seq').astype(jnp.bfloat16)]
    ppermute x0 -> x2, waiting for transfers between devices: none -> 6.31 us  [the longest x1 6.3 us: per_device(): kvs = [partial, lax.ppermute(partial, 'seq', swap)]]
    all_to_all x0 -> x1, starting transfers between devices: none -> 5.99 us  [per_device(): spread = lax.all_to_all(flat, 'dp', split_axis=1, concat_axis=0, tiled=True)]
    all_gather x1 -> x0, blocking collectives: 4.94 us -> none  [per_device(): key_value = lax.all_gather(own_rows[None], 'seq', axis=1, tiled=True)]
  transfers between devices with their start and end apart: 2 -> 5, of which waited for: 2 -> 4; matrix products, arithmetic and copies ran while one was open for 4% -> 6% of each run, Pallas kernels for 0% -> 0%
where the time goes in v1:
time: 155 us
  waiting for transfers between devices  106 us (68%)
  between operations  14.1 us (9%)
  local copies, waits for them, and re-layouts  13.6 us (9%)
  starting transfers between devices  10.8 us (7%)
  matrix products  5.96 us (4%)
  Pallas kernels  3.23 us (2%)
    all_to_all x1, waiting for transfers between devices, per_device(): spread = lax.all_to_all(flat, 'dp', split_axis=1, concat_axis=0, tiled=True)  44.6 us
    all_gather x1, waiting for transfers between devices, per_device(): weight_grad = lax.all_gather(piece, 'dp', axis=0, tiled=True)  43.2 us
    all_gather x1, waiting for transfers between devices, per_device(): all_grads = lax.all_gather(grad_kv, 'dp', axis=0, tiled=True)  12.1 us
    unnamed x12, local copies, waits for them, and re-layouts  9.71 us
    ppermute x1, waiting for transfers between devices, per_device(): kvs = [partial, lax.ppermute(partial, 'seq', swap)]  6.3 us
    all_to_all x1, starting transfers between devices, per_device(): spread = lax.all_to_all(flat, 'dp', split_axis=1, concat_axis=0, tiled=True)  5.99 us
    all_to_all x1, local copies, waits for them, and re-layouts, per_device(): spread = lax.all_to_all(flat, 'dp', split_axis=1, concat_axis=0, tiled=True)  3.9 us
    dot_general x1, matrix products, _mm(): return lax.dot_general(a, b, dims, preferred_element_type=F32)  3.62 us
  transfers between devices with their start and end apart: 5, of which 4 were waited for; matrix products, arithmetic and copies ran while one was open for 6% of the time, Pallas kernels for 0%

profile of v1, /device:TPU:0, one launch (start us, length us, event | category | flops | bytes accessed | tf_op | source)
XLA Modules:
  0.0 154.6 jit_solution(16210178644109728954)
XLA Ops:
  7.2 0.0 copy-start
  7.2 0.0 copy-start.4
  7.2 0.0 copy-start.3
  7.2 0.0 copy-start.2
  7.2 1.6 %copy-done = bf16[4096,256]{1,0:T(8,128)(2,1)S(1)} copy-done((bf16[4096,256]{1,0:T(8,128)(2,1)S(1)}, bf16[4096,256]{1,0:T(8,128)(2,1)}, u32[]{:S(2)}) %copy-start) | copy-done | bytes 2097176
  8.8 0.0 copy-start.1
  8.8 2.3 %fusion.refs_0_ = f32[256,256]{1,0:T(8,128)S(1)} fusion(bf16[4096,256]{1,0:T(8,128)(2,1)S(1)} %copy-done, bf16[1,256,4096]{2,1,0:T(8,128)(2,1)} %param.6), kind=kOutput, calls=%fused_computation | convolution fusion | flops 536870912 | bytes 4456448 | tf_op jit(solution)/shard_map/dot_general | solution.py:104
  11.1 3.0 %collective-permute-start = (f32[256,256]{1,0:T(8,128)S(1)}, f32[256,256]{1,0:T(8,128)S(1)}, u32[]{:S(2)}, u32[]{:S(2)}) collective-permute-start(f32[256,256]{1,0:T(8,128)S(1)} %fusion.refs_0_), channel_id=1, source_target_pairs={{0,1},{1,0},{2,3},{3,2},{4,5},{5,4},{6,7},{7,6},{8,9},{9,8},{10,11... | collective-permute-start | bytes 786440 | tf_op jit(solution)/shard_map/ppermute | solution.py:107
  14.1 6.3 %collective-permute-done.refs_1_ = f32[256,256]{1,0:T(8,128)S(1)} collective-permute-done((f32[256,256]{1,0:T(8,128)S(1)}, f32[256,256]{1,0:T(8,128)S(1)}, u32[]{:S(2)}, u32[]{:S(2)}) %collective-permute-start) | collective-permute-done | bytes 262176 | tf_op jit(solution)/shard_map/ppermute | solution.py:107
  20.4 0.0 copy-done.4
  20.4 0.0 copy-done.3
  20.4 0.0 copy-done.2
  20.4 0.0 copy-done.1
  20.4 3.2 %attention_fwd_bwd.1 = (bf16[128,1024]{1,0:T(8,128)(2,1)}, bf16[128,1024]{1,0:T(8,128)(2,1)}, f32[256,256]{1,0:T(8,128)S(1)}) custom-call(s32[2]{0:T(128)S(1)} %copy-done.4, s32[2,128]{1,0:T(2,128)S(1)} %bitcast.18, bf16[128,1024]{1,0:T(8,128)(2,1)S(1)} %bitcast.16, bf16[128,1024]{1,0:T(8,128)(2,1)S(1)} %bitcast.17, f32[256,256]{1,0:T(8,128)S(1)} %fusion.refs_0_, ...), custom_call_target="tpu_custom_call" | custom-call | tf_op jit(solution)/shard_map/attention_fwd_bwd/pallas_call | solution.py:84
  23.7 1.7 %collective-permute-start.1 = (f32[256,256]{1,0:T(8,128)S(1)}, f32[256,256]{1,0:T(8,128)S(1)}, u32[]{:S(2)}, u32[]{:S(2)}) collective-permute-start(f32[256,256]{1,0:T(8,128)S(1)} %get-tuple-element.8), channel_id=1, source_target_pairs={{0,1},{1,0},{2,3},{3,2},{4,5},{5,4},{6,7},{7,6},{8,9},{9,8},{10,11... | collective-permute-start | bytes 786440 | tf_op jit(solution)/shard_map/ppermute | solution.py:114
  25.4 4.1 %copy.11 = bf16[1,256,4096]{1,2,0:T(8,128)(2,1)} copy(bf16[1,256,4096]{2,1,0:T(8,128)(2,1)} %param.6) | data formatting | bytes 4194304 | tf_op args[0]
  29.5 6.0 %all-to-all-start = ((bf16[256,16,256]{0,2,1:T(8,128)(2,1)}), bf16[256,16,256]{0,2,1:T(8,128)(2,1)}, u32[]{:S(2)}, u32[]{:S(2)}) async-start(bf16[256,16,256]{0,2,1:T(8,128)(2,1)} %bitcast.19), calls=%async_computation | async-start | bytes 4194304 | tf_op jit(solution)/shard_map/all_to_all | solution.py:103
  35.5 0.0 all-gather.3.cloned.1.call-start
  35.5 0.0 collective-permute-done.1
  35.5 0.7 add_convert_fusion
  36.2 0.0 all-gather.3.cloned.1.call-update
  36.2 0.0 all-gather.5.cloned.1.call-start
  36.3 44.6 %all-to-all-done = bf16[256,16,256]{0,2,1:T(8,128)(2,1)} async-done(((bf16[256,16,256]{0,2,1:T(8,128)(2,1)}), bf16[256,16,256]{0,2,1:T(8,128)(2,1)}, u32[]{:S(2)}, u32[]{:S(2)}) %all-to-all-start) | async-done | bytes 2097184 | tf_op jit(solution)/shard_map/all_to_all | solution.py:103
  80.9 3.9 %copy.12 = bf16[16,256,256]{2,1,0:T(8,128)(2,1)} copy(bf16[16,256,256]{1,2,0:T(8,128)(2,1)} %bitcast.7) | data formatting | bytes 4194304 | tf_op jit(solution)/shard_map/all_to_all | solution.py:103
  84.8 12.1 %all-gather.3.cloned.1.call-done = bf16[4096,256]{1,0:T(8,128)(2,1)} async-done(((bf16[256,256]{1,0:T(8,128)(2,1)}), bf16[4096,256]{1,0:T(8,128)(2,1)}) %all-gather.3.cloned.1.call-update) | async-done | bytes 2097168 | tf_op jit(solution)/shard_map/all_gather | solution.py:117
  96.9 3.6 %fusion.3 = bf16[256,256]{0,1:T(8,128)(2,1)} fusion(bf16[4096,256]{1,0:T(8,128)(2,1)} %all-gather.3.cloned.1.call-done, bf16[4096,256]{1,0:T(8,128)(2,1)} %bitcast.20), kind=kOutput, calls=%fused_computation.4 | convolution fusion | flops 537001984 | bytes 4325376 | tf_op jit(solution)/shard_map/dot_general | solution.py:22
  100.5 0.0 all-gather.5.cloned.1.call-update
  100.5 43.2 %all-gather.5.cloned.1.call-done = bf16[4096,256]{0,1:T(8,128)(2,1)} async-done(((bf16[256,256]{0,1:T(8,128)(2,1)}), bf16[4096,256]{0,1:T(8,128)(2,1)}) %all-gather.5.cloned.1.call-update) | async-done | bytes 2097168 | tf_op jit(solution)/shard_map/all_gather | solution.py:120
  143.7 4.1 %copy.13 = bf16[4096,256]{1,0:T(8,128)(2,1)} copy(bf16[4096,256]{0,1:T(8,128)(2,1)} %all-gather.5.cloned.1.call-done) | data formatting | bytes 4194304
Async XLA Ops:
  7.2 1.6 %copy-start = (bf16[4096,256]{1,0:T(8,128)(2,1)S(1)}, bf16[4096,256]{1,0:T(8,128)(2,1)}, u32[]{:S(2)}) copy-start(bf16[4096,256]{1,0:T(8,128)(2,1)} %param.9) | copy-start | bytes 6291460
  7.2 13.2 %copy-start.4 = (s32[2]{0:T(128)S(1)}, s32[2]{0:T(128)}, u32[]{:S(2)}) copy-start(s32[2]{0:T(128)} %order_ref.1) | copy-start | bytes 28
  7.2 13.2 %copy-start.3 = (s32[1,256]{1,0:T(1,128)S(1)}, s32[1,256]{1,0:T(1,128)}, u32[]{:S(2)}) copy-start(s32[1,256]{1,0:T(1,128)} %param.10) | copy-start | bytes 3076
  7.2 13.2 %copy-start.2 = (bf16[1,128,1024]{2,1,0:T(8,128)(2,1)S(1)}, bf16[1,128,1024]{2,1,0:T(8,128)(2,1)}, u32[]{:S(2)}) copy-start(bf16[1,128,1024]{2,1,0:T(8,128)(2,1)} %param.8) | copy-start | bytes 786436
  8.8 11.7 %copy-start.1 = (bf16[1,128,1024]{2,1,0:T(8,128)(2,1)S(1)}, bf16[1,128,1024]{2,1,0:T(8,128)(2,1)}, u32[]{:S(2)}) copy-start(bf16[1,128,1024]{2,1,0:T(8,128)(2,1)} %param.7) | copy-start | bytes 786436
  11.1 9.3 %collective-permute-start = (f32[256,256]{1,0:T(8,128)S(1)}, f32[256,256]{1,0:T(8,128)S(1)}, u32[]{:S(2)}, u32[]{:S(2)}) collective-permute-start(f32[256,256]{1,0:T(8,128)S(1)} %fusion.refs_0_), channel_id=1, source_target_pairs={{0,1},{1,0},{2,3},{3,2},{4,5},{5,4},{6,7},{7,6},{8,9},{9,8},{10,11... | collective-permute-start | bytes 786440 | tf_op jit(solution)/shard_map/ppermute | solution.py:107
  23.7 11.9 %collective-permute-start.1 = (f32[256,256]{1,0:T(8,128)S(1)}, f32[256,256]{1,0:T(8,128)S(1)}, u32[]{:S(2)}, u32[]{:S(2)}) collective-permute-start(f32[256,256]{1,0:T(8,128)S(1)} %get-tuple-element.8), channel_id=1, source_target_pairs={{0,1},{1,0},{2,3},{3,2},{4,5},{5,4},{6,7},{7,6},{8,9},{9,8},{10,11... | collective-permute-start | bytes 786440 | tf_op jit(solution)/shard_map/ppermute | solution.py:114
  29.5 51.4 %all-to-all-start = ((bf16[256,16,256]{0,2,1:T(8,128)(2,1)}), bf16[256,16,256]{0,2,1:T(8,128)(2,1)}, u32[]{:S(2)}, u32[]{:S(2)}) async-start(bf16[256,16,256]{0,2,1:T(8,128)(2,1)} %bitcast.19), calls=%async_computation | async-start | bytes 4194304 | tf_op jit(solution)/shard_map/all_to_all | solution.py:103
  35.5 61.4 %all-gather.3.cloned.1.call-start = ((), (), s32[]{:S(2)}) async-start(), calls=%async_computation.1 | async-start | bytes 2228224 | tf_op jit(solution)/shard_map/all_gather | solution.py:117
  36.2 107.5 %all-gather.5.cloned.1.call-start = ((), (), s32[]{:S(2)}) async-start(), calls=%async_computation.2 | async-start | bytes 2228224 | tf_op jit(solution)/shard_map/all_gather | solution.py:120
Sparse Core Ops, SparseCore 0:
  38.5 58.3 all-gather.2
  100.6 43.0 all-gather.4
